TPU v7x, 32 devices: a whole 2x2x4 slice. The times are simulated.
32 devices in a mesh: grp: 2 (over y), row: 4 (over z), col: 2 (over x), pair: 2 (over core).
Axes of the slice: x: 2, y: 2, z: 4, core: 2. Of those that a mesh axis runs over, the one named last changes fastest.
Arguments:
- features_in: bfloat16 [128, 32, 512], P('grp', 'row', ('col', 'pair')), parts along dimension 0, may hold values from -8 to 8
- filters_one: bfloat16 [64, 3, 3, 64], replicated, may hold values from -0.25 to 0.25
- filters_two: bfloat16 [512, 3, 3, 256], P('row'), may hold values from -0.125 to 0.125
- out_grad: bfloat16 [1024, 128, 8], P(('grp', 'row'), ('col', 'pair')), parts along dimension 0, may hold values from -24 to 24
Outputs:
- input_grad: bfloat16 [128, 32, 512], P('grp', 'row', ('col', 'pair')), parts along dimension 0
- grad_one: float32 [128, 3, 3, 64], P('grp'), parts along dimension 0
- grad_two: float32 [1024, 3, 3, 256], P(('grp', 'row')), parts along dimension 0
There are 2 independent parts, one for each index of `grp`. A program takes and returns all parts, laid end to end along the dimension named above; an argument that names none is the same for every part. Nothing has to cross between parts.
All inputs are finite; a program needn't handle non-finite values.
Results may differ from a plain program's by a relative error of at most 0.015.
Values may be sent and summed in bfloat16 or wider, within the bound.
A program may use at most 64 MiB of HBM per device.

v0:
```python
import math
import jax
import jax.numpy as jnp
from jax import lax
from jax.sharding import PartitionSpec as P


def padded_2(cells, sides, width):
    for axis, dim in sides:
        count = lax.axis_size(axis)
        ends = count - 1
        head = lax.slice_in_dim(cells, 0, width, axis=dim)
        tail = lax.slice_in_dim(cells, cells.shape[dim] - width, cells.shape[dim], axis=dim)
        cells = jnp.concatenate(
            [
                lax.ppermute(tail, axis, [(i, (i + 1) % count) for i in range(ends)]),
                cells,
                lax.ppermute(head, axis, [((i + 1) % count, i) for i in range(ends)]),
            ],
            axis=dim,
        )
    return cells


def conv_valid(padded, kernel):
    return lax.conv_general_dilated(
        padded[None],
        kernel,
        (1, 1),
        "VALID",
        dimension_numbers=("NCHW", "OHWI", "NCHW"),
        preferred_element_type=jnp.float32,
    )[0]


def flip_kernel(kernel):
    return jnp.transpose(kernel[:, ::-1, ::-1, :], (3, 1, 2, 0))


def silu_slope(values):
    sigmoid_value = jax.nn.sigmoid(values)
    return sigmoid_value * (1.0 + values * (1.0 - sigmoid_value))


def tap_grads(gradient, padded):
    row_count, col_count = (gradient.shape[1], gradient.shape[2])
    tap_list = []
    for first_tap in range(3):
        tap_row = []
        for second_tap in range(3):
            window = padded[
                :, first_tap : first_tap + row_count, second_tap : second_tap + col_count
            ]
            tap_row.append(
                jnp.einsum("ohw,chw->oc", gradient, window, preferred_element_type=jnp.float32)
            )
        tap_list.append(jnp.stack(tap_row, 1))
    return jnp.stack(tap_list, 1)


def pool_columns(active):
    channels, row_count, col_count = active.shape
    folded = active.reshape(channels, row_count // 4, 2, 2, col_count // 4, 2, 2).mean(axis=(3, 6))
    return jnp.transpose(folded, (0, 2, 4, 3, 1)).reshape(
        channels * 4, col_count // 4, row_count // 4
    )


def unpool_columns(gradient):
    quad_count, col_count, row_count = gradient.shape
    ordered = jnp.transpose(
        gradient.reshape(quad_count // 4, 2, 2, col_count, row_count), (0, 4, 1, 3, 2)
    )
    spread = (
        jnp.broadcast_to(
            ordered[:, :, :, None, :, :, None], (quad_count // 4, row_count, 2, 2, col_count, 2, 2)
        )
        * 0.25
    )
    return spread.reshape(quad_count // 4, row_count * 4, col_count * 4)


def local(features_in, filters_one, filters_two, out_grad):
    band_rows = features_in.shape[1]
    strip_cols = features_in.shape[2]
    height = band_rows * lax.axis_size("row")
    width = strip_cols * lax.axis_size(("col", "pair"))
    padded_in = padded_2(features_in, (("row", 1), (("col", "pair"), 2)), 1)
    pre_one = conv_valid(padded_in, filters_one)
    pooled = pool_columns(jax.nn.silu(pre_one)).astype(jnp.bfloat16)
    with_edges = padded_2(pooled, ((("col", "pair"), 1),), 1)
    column_strip = lax.all_gather(with_edges, "row", axis=2, tiled=True)
    strip_padded = jnp.pad(column_strip, ((0, 0), (0, 0), (1, 1)))
    swapped = jnp.transpose(filters_two, (0, 2, 1, 3))
    pre_two = conv_valid(strip_padded, swapped)
    grad_pre_two = (out_grad.astype(jnp.float32) * silu_slope(pre_two)).astype(jnp.bfloat16)
    pooled_height = column_strip.shape[2]
    pooled_width = strip_cols // 4 * lax.axis_size(("col", "pair"))
    local_two = jnp.transpose(tap_grads(grad_pre_two, strip_padded), (0, 2, 1, 3))
    grad_two = lax.psum(local_two, ("col", "pair")) / math.sqrt(pooled_height * pooled_width)
    padded_grad = jnp.pad(grad_pre_two, ((0, 0), (2, 2), (1, 1)))
    spread_grad = conv_valid(padded_grad, flip_kernel(swapped))
    with_ghosts = padded_2(spread_grad, ((("col", "pair"), 1),), 1)
    real_columns = spread_grad[:, 1:-1, :]
    real_columns = real_columns.at[:, 0, :].add(with_ghosts[:, 0, :])
    real_columns = real_columns.at[:, -1, :].add(with_ghosts[:, -1, :])
    grad_pooled = lax.psum_scatter(real_columns, "row", scatter_dimension=2, tiled=True)
    grad_pre_one = (unpool_columns(grad_pooled) * silu_slope(pre_one)).astype(jnp.bfloat16)
    local_one = tap_grads(grad_pre_one, padded_in)
    grad_one = lax.psum(local_one, ("row", "col", "pair")) / math.sqrt(height * width)
    rimmed_one = padded_2(grad_pre_one, (("row", 1), (("col", "pair"), 2)), 1)
    input_grad = conv_valid(rimmed_one, flip_kernel(filters_one)).astype(jnp.bfloat16)
    return (input_grad, grad_one, grad_two)


def solution(mesh):
    in_specs = (
        P("grp", "row", ("col", "pair")),
        P(),
        P("row", None, None, None),
        P(("grp", "row"), ("col", "pair"), None),
    )
    out_specs = (
        P("grp", "row", ("col", "pair")),
        P("grp", None, None, None),
        P(("grp", "row"), None, None, None),
    )
    return jax.shard_map(local, mesh=mesh, in_specs=in_specs, out_specs=out_specs, check_vma=False)
```

profile of v0, /device:TPU:0, one launch (start us, length us, event | category | flops | bytes accessed | tf_op | source)
XLA Modules:
  0.0 211.8 jit_solution(14888131075437018906)
XLA Ops:
  8.1 1.0 copy.216
  9.1 4.9 %collective-permute-start = (bf16[64,1,128]{2,0,1:T(8,128)(2,1)S(1)}, bf16[64,1,128]{2,0,1:T(8,128)(2,1)S(1)}, u32[]{:S(2)}, u32[]{:S(2)}) collective-permute-start(bf16[64,1,128]{2,0,1:T(8,128)(2,1)S(1)} %get-tuple-element.58), channel_id=1, source_target_pairs={{0,4},{4,8},{8,12},{1,5},{5,9},{9,13},{2,6},{6,10},{10,14},{3,7},{... | collective-permute-start | bytes 49160 | tf_op jit(solution)/shard_map/ppermute | solution.py:16
  14.0 1.3 collective-permute-start.1
  15.4 0.9 constant_dynamic-update-slice_fusion.1
  16.4 3.3 %collective-permute-done.1 = bf16[64,1,128]{2,0,1:T(8,128)(2,1)S(1)} collective-permute-done((bf16[64,1,128]{2,0,1:T(8,128)(2,1)S(1)}, bf16[64,1,128]{2,0,1:T(8,128)(2,1)S(1)}, u32[]{:S(2)}, u32[]{:S(2)}) %collective-permute-start.1) | collective-permute-done | bytes 16416 | tf_op jit(solution)/shard_map/ppermute | solution.py:18
  19.7 1.3 collective-permute-start.3
  21.0 3.0 %collective-permute-start.2 = (bf16[64,10,1]{2,0,1:T(8,128)(2,1)S(1)}, bf16[64,10,1]{2,0,1:T(8,128)(2,1)S(1)}, u32[]{:S(2)}, u32[]{:S(2)}) collective-permute-start(bf16[64,10,1]{2,0,1:T(8,128)(2,1)S(1)} %get-tuple-element.51), channel_id=1, source_target_pairs={{0,1},{1,2},{2,3},{4,5},{5,6},{6,7},{8,9},{9,10},{10,11},{12,13},{... | collective-permute-start | bytes 3848 | tf_op jit(solution)/shard_map/ppermute | solution.py:16
  24.1 1.0 collective-permute-done.2
  26.5 0.8 convolution_select_fusion.1
  27.6 0.9 fusion.3
  28.8 1.3 collective-permute-start.5
  30.1 4.9 %collective-permute-start.4 = (bf16[256,1,2]{1,0,2:T(8,128)(2,1)S(1)}, bf16[256,1,2]{1,0,2:T(8,128)(2,1)S(1)}, u32[]{:S(2)}, u32[]{:S(2)}) collective-permute-start(bf16[256,1,2]{1,0,2:T(8,128)(2,1)S(1)} %get-tuple-element.55), channel_id=1, source_target_pairs={{0,1},{1,2},{2,3},{4,5},{5,6},{6,7},{8,9},{9,10},{10,11},{12,13},{... | collective-permute-start | bytes 3080 | tf_op jit(solution)/shard_map/ppermute | solution.py:16
  36.2 13.7 %all_gather.3 = bf16[256,34,8]{0,1,2:T(8,128)(2,1)S(1)} all-gather(bf16[256,34,2]{0,1,2:T(8,128)(2,1)S(1)} %copy.226), channel_id=1, replica_groups=mesh['grp'=2,'row'=4,'col'=2,'pair'=2] {'row'}, dimensions={2}, use_global_device_ids=true | all-gather | bytes 174080 | tf_op jit(solution)/shard_map/all_gather | solution.py:92
  50.1 1.0 fusion.6
  52.8 1.0 fusion.4
  53.9 2.4 %collective-permute-start.6 = (f32[256,1,8]{0,2,1:T(8,128)S(1)}, f32[256,1,8]{0,2,1:T(8,128)S(1)}, u32[]{:S(2)}, u32[]{:S(2)}) collective-permute-start(f32[256,1,8]{0,2,1:T(8,128)S(1)} %get-tuple-element.48), channel_id=1, source_target_pairs={{0,1},{1,2},{2,3},{4,5},{5,6},{6,7},{8,9},{9,10},{10,11},{12,13},{... | collective-permute-start | bytes 24584 | tf_op jit(solution)/shard_map/ppermute | solution.py:16
  56.6 1.3 collective-permute-start.7
  57.9 6.6 %collective-permute-done.7 = f32[256,1,8]{0,2,1:T(8,128)S(1)} collective-permute-done((f32[256,1,8]{0,2,1:T(8,128)S(1)}, f32[256,1,8]{0,2,1:T(8,128)S(1)}, u32[]{:S(2)}, u32[]{:S(2)}) %collective-permute-start.7) | collective-permute-done | bytes 8224 | tf_op jit(solution)/shard_map/ppermute | solution.py:18
  65.7 1.1 maximum_bitcast_fusion
  66.8 18.7 %reduce-scatter.2.cloned.1.call-done = f32[256,32,2]{0,1,2:T(8,128)} async-done(((f32[256,32,8]{0,1,2:T(8,128)}), f32[256,32,2]{0,1,2:T(8,128)}) %reduce-scatter.2.cloned.1.call-update) | async-done | bytes 65552 | tf_op jit(solution)/shard_map/reduce_scatter | solution.py:107
  85.5 0.8 broadcast_multiply_fusion.2
  87.7 1.3 collective-permute-start.8
  89.0 1.3 collective-permute-start.9
  92.4 2.4 %collective-permute-done.9 = bf16[64,1,128]{2,1,0:T(2,128)(2,1)S(1)} collective-permute-done((bf16[64,1,128]{2,1,0:T(2,128)(2,1)S(1)}, bf16[64,1,128]{2,1,0:T(2,128)(2,1)S(1)}, u32[]{:S(2)}, u32[]{:S(2)}) %collective-permute-start.9) | collective-permute-done | bytes 16416 | tf_op jit(solution)/shard_map/ppermute | solution.py:18
  94.9 1.3 collective-permute-start.11
  96.2 3.0 %collective-permute-start.10 = (bf16[64,10,1]{2,0,1:T(8,128)(2,1)S(1)}, bf16[64,10,1]{2,0,1:T(8,128)(2,1)S(1)}, u32[]{:S(2)}, u32[]{:S(2)}) collective-permute-start(bf16[64,10,1]{2,0,1:T(8,128)(2,1)S(1)} %get-tuple-element.49), channel_id=1, source_target_pairs={{0,1},{1,2},{2,3},{4,5},{5,6},{6,7},{8,9},{9,10},{10,11},{12,13},{... | collective-permute-start | bytes 3848 | tf_op jit(solution)/shard_map/ppermute | solution.py:16
  101.7 0.9 copy.259
  102.6 5.7 %all-reduce.7.cloned.1.call-done = f32[128,3,3,256]{3,0,1,2:T(8,128)} async-done(((f32[128,3,3,256]{3,0,1,2:T(8,128)}), f32[128,3,3,256]{3,0,1,2:T(8,128)}) %all-reduce.7.cloned.1.call-update) | async-done | bytes 1179664 | tf_op jit(solution)/shard_map/psum | solution.py:100
  108.3 1.4 broadcast_multiply_fusion
  109.7 1.1 copy.260
  110.8 91.9 %all-reduce.5.cloned.1.call-done = f32[64,3,3,64]{3,0,2,1:T(8,128)} async-done(((f32[64,3,3,64]{3,0,2,1:T(8,128)}), f32[64,3,3,64]{3,0,2,1:T(8,128)}) %all-reduce.5.cloned.1.call-update) | async-done | bytes 147472 | tf_op jit(solution)/shard_map/psum | solution.py:110
  202.6 1.7 broadcast_multiply_fusion.1
  (95 shorter events, 12.5 us)
Async XLA Ops:
  8.0 42.1 %copy-start = (bf16[128,3,3,256]{3,0,2,1:T(8,128)(2,1)S(1)}, bf16[128,3,3,256]{3,0,2,1:T(8,128)(2,1)}, u32[]{:S(2)}) copy-start(bf16[128,3,3,256]{3,0,2,1:T(8,128)(2,1)} %param.10) | copy-start | bytes 1769476
  8.0 77.5 %reduce-scatter.2.cloned.1.call-start = ((), (), s32[]{:S(2)}) async-start(), calls=%async_computation.1 | async-start | bytes 327680 | tf_op jit(solution)/shard_map/reduce_scatter | solution.py:107
  9.1 6.4 %collective-permute-start = (bf16[64,1,128]{2,0,1:T(8,128)(2,1)S(1)}, bf16[64,1,128]{2,0,1:T(8,128)(2,1)S(1)}, u32[]{:S(2)}, u32[]{:S(2)}) collective-permute-start(bf16[64,1,128]{2,0,1:T(8,128)(2,1)S(1)} %get-tuple-element.58), channel_id=1, source_target_pairs={{0,4},{4,8},{8,12},{1,5},{5,9},{9,13},{2,6},{6,10},{10,14},{3,7},{... | collective-permute-start | bytes 49160 | tf_op jit(solution)/shard_map/ppermute | solution.py:16
  14.0 5.6 %collective-permute-start.1 = (bf16[64,1,128]{2,0,1:T(8,128)(2,1)S(1)}, bf16[64,1,128]{2,0,1:T(8,128)(2,1)S(1)}, u32[]{:S(2)}, u32[]{:S(2)}) collective-permute-start(bf16[64,1,128]{2,0,1:T(8,128)(2,1)S(1)} %get-tuple-element.57), channel_id=1, source_target_pairs={{4,0},{8,4},{12,8},{5,1},{9,5},{13,9},{6,2},{10,6},{14,10},{7,3},{... | collective-permute-start | bytes 49160 | tf_op jit(solution)/shard_map/ppermute | solution.py:18
  19.7 4.4 %collective-permute-start.3 = (bf16[64,10,1]{2,0,1:T(8,128)(2,1)S(1)}, bf16[64,10,1]{2,0,1:T(8,128)(2,1)S(1)}, u32[]{:S(2)}, u32[]{:S(2)}) collective-permute-start(bf16[64,10,1]{2,0,1:T(8,128)(2,1)S(1)} %get-tuple-element.52), channel_id=1, source_target_pairs={{1,0},{2,1},{3,2},{5,4},{6,5},{7,6},{9,8},{10,9},{11,10},{13,12},{... | collective-permute-start | bytes 3848 | tf_op jit(solution)/shard_map/ppermute | solution.py:18
  21.0 4.0 %collective-permute-start.2 = (bf16[64,10,1]{2,0,1:T(8,128)(2,1)S(1)}, bf16[64,10,1]{2,0,1:T(8,128)(2,1)S(1)}, u32[]{:S(2)}, u32[]{:S(2)}) collective-permute-start(bf16[64,10,1]{2,0,1:T(8,128)(2,1)S(1)} %get-tuple-element.51), channel_id=1, source_target_pairs={{0,1},{1,2},{2,3},{4,5},{5,6},{6,7},{8,9},{9,10},{10,11},{12,13},{... | collective-permute-start | bytes 3848 | tf_op jit(solution)/shard_map/ppermute | solution.py:16
  25.6 0.9 copy-start.3
  25.6 0.9 copy-start.4
  28.8 6.4 %collective-permute-start.5 = (bf16[256,1,2]{1,0,2:T(8,128)(2,1)S(1)}, bf16[256,1,2]{1,0,2:T(8,128)(2,1)S(1)}, u32[]{:S(2)}, u32[]{:S(2)}) collective-permute-start(bf16[256,1,2]{1,0,2:T(8,128)(2,1)S(1)} %get-tuple-element.56), channel_id=1, source_target_pairs={{1,0},{2,1},{3,2},{5,4},{6,5},{7,6},{9,8},{10,9},{11,10},{13,12},{... | collective-permute-start | bytes 3080 | tf_op jit(solution)/shard_map/ppermute | solution.py:18
  30.1 5.9 %collective-permute-start.4 = (bf16[256,1,2]{1,0,2:T(8,128)(2,1)S(1)}, bf16[256,1,2]{1,0,2:T(8,128)(2,1)S(1)}, u32[]{:S(2)}, u32[]{:S(2)}) collective-permute-start(bf16[256,1,2]{1,0,2:T(8,128)(2,1)S(1)} %get-tuple-element.55), channel_id=1, source_target_pairs={{0,1},{1,2},{2,3},{4,5},{5,6},{6,7},{8,9},{9,10},{10,11},{12,13},{... | collective-permute-start | bytes 3080 | tf_op jit(solution)/shard_map/ppermute | solution.py:16
  50.1 1.0 copy-start.2
  53.9 4.0 %collective-permute-start.6 = (f32[256,1,8]{0,2,1:T(8,128)S(1)}, f32[256,1,8]{0,2,1:T(8,128)S(1)}, u32[]{:S(2)}, u32[]{:S(2)}) collective-permute-start(f32[256,1,8]{0,2,1:T(8,128)S(1)} %get-tuple-element.48), channel_id=1, source_target_pairs={{0,1},{1,2},{2,3},{4,5},{5,6},{6,7},{8,9},{9,10},{10,11},{12,13},{... | collective-permute-start | bytes 24584 | tf_op jit(solution)/shard_map/ppermute | solution.py:16
  56.6 7.9 %collective-permute-start.7 = (f32[256,1,8]{0,2,1:T(8,128)S(1)}, f32[256,1,8]{0,2,1:T(8,128)S(1)}, u32[]{:S(2)}, u32[]{:S(2)}) collective-permute-start(f32[256,1,8]{0,2,1:T(8,128)S(1)} %get-tuple-element.47), channel_id=1, source_target_pairs={{1,0},{2,1},{3,2},{5,4},{6,5},{7,6},{9,8},{10,9},{11,10},{13,12},{... | collective-permute-start | bytes 24584 | tf_op jit(solution)/shard_map/ppermute | solution.py:18
  65.3 43.0 %all-reduce.7.cloned.1.call-start = ((), (), s32[]{:S(2)}) async-start(), calls=%async_computation.3 | async-start | bytes 2359296 | tf_op jit(solution)/shard_map/psum | solution.py:100
  66.8 135.9 %all-reduce.5.cloned.1.call-start = ((), (), s32[]{:S(2)}) async-start(), calls=%async_computation.2 | async-start | bytes 589824 | tf_op jit(solution)/shard_map/psum | solution.py:110
  86.6 0.9 copy-start.1
  87.7 4.6 %collective-permute-start.8 = (bf16[64,1,128]{2,1,0:T(2,128)(2,1)S(1)}, bf16[64,1,128]{2,1,0:T(2,128)(2,1)S(1)}, u32[]{:S(2)}, u32[]{:S(2)}) collective-permute-start(bf16[64,1,128]{2,1,0:T(2,128)(2,1)S(1)} %get-tuple-element.54), channel_id=1, source_target_pairs={{0,4},{4,8},{8,12},{1,5},{5,9},{9,13},{2,6},{6,10},{10,14},{3,7},{... | collective-permute-start | bytes 49160 | tf_op jit(solution)/shard_map/ppermute | solution.py:16
  89.0 5.8 %collective-permute-start.9 = (bf16[64,1,128]{2,1,0:T(2,128)(2,1)S(1)}, bf16[64,1,128]{2,1,0:T(2,128)(2,1)S(1)}, u32[]{:S(2)}, u32[]{:S(2)}) collective-permute-start(bf16[64,1,128]{2,1,0:T(2,128)(2,1)S(1)} %get-tuple-element.53), channel_id=1, source_target_pairs={{4,0},{8,4},{12,8},{5,1},{9,5},{13,9},{6,2},{10,6},{14,10},{7,3},{... | collective-permute-start | bytes 49160 | tf_op jit(solution)/shard_map/ppermute | solution.py:18
  94.9 5.1 %collective-permute-start.11 = (bf16[64,10,1]{2,0,1:T(8,128)(2,1)S(1)}, bf16[64,10,1]{2,0,1:T(8,128)(2,1)S(1)}, u32[]{:S(2)}, u32[]{:S(2)}) collective-permute-start(bf16[64,10,1]{2,0,1:T(8,128)(2,1)S(1)} %get-tuple-element.50), channel_id=1, source_target_pairs={{1,0},{2,1},{3,2},{5,4},{6,5},{7,6},{9,8},{10,9},{11,10},{13,12},{... | collective-permute-start | bytes 3848 | tf_op jit(solution)/shard_map/ppermute | solution.py:18
  96.2 4.0 %collective-permute-start.10 = (bf16[64,10,1]{2,0,1:T(8,128)(2,1)S(1)}, bf16[64,10,1]{2,0,1:T(8,128)(2,1)S(1)}, u32[]{:S(2)}, u32[]{:S(2)}) collective-permute-start(bf16[64,10,1]{2,0,1:T(8,128)(2,1)S(1)} %get-tuple-element.49), channel_id=1, source_target_pairs={{0,1},{1,2},{2,3},{4,5},{5,6},{6,7},{8,9},{9,10},{10,11},{12,13},{... | collective-permute-start | bytes 3848 | tf_op jit(solution)/shard_map/ppermute | solution.py:16
Sparse Core Ops, SparseCore 0:
  65.4 20.0 reduce-scatter.1
Sparse Core Ops, SparseCore 1:
  68.8 39.4 all-reduce.6
  112.5 90.1 all-reduce.4
where the time goes:
time: 212 us
  waiting for transfers between devices  131 us (62%)
  starting transfers between devices  27.5 us (13%)
  between operations  16.1 us (8%)
  blocking collectives  13.7 us (6%)
  local copies, waits for them, and re-layouts  8.75 us (4%)
  other arithmetic  7.58 us (4%)
  matrix products  7.49 us (4%)
    psum x1, waiting for transfers between devices, local(): lax.psum(local_one, ('row', 'col', 'pair')) / math.sqrt(height * width)  91.9 us
    ppermute x6, starting transfers between devices, padded_2(): lax.ppermute(tail, axis, [(i, (i + 1) % count) for i in range(ends)])  19.6 us
    reduce_scatter x1, waiting for transfers between devices, local(): lax.psum_scatter(real_columns, 'row', scatter_dimension=2, tiled=True)  18.7 us
    all_gather x1, blocking collectives, local(): column_strip = lax.all_gather(with_edges, 'row', axis=2, tiled=True)  13.7 us
    ppermute x6, waiting for transfers between devices, padded_2(): lax.ppermute(head, axis, [((i + 1) % count, i) for i in range(ends)])  12.2 us
    ppermute x6, starting transfers between devices, padded_2(): lax.ppermute(head, axis, [((i + 1) % count, i) for i in range(ends)])  7.75 us
    psum x1, waiting for transfers between devices, local(): lax.psum(local_two, ('col', 'pair'))  5.73 us
    unnamed x21, local copies, waits for them, and re-layouts  5.7 us
  transfers between devices with their start and end apart: 15, of which 10 were waited for; matrix products, arithmetic and copies ran while one was open for 6% of the time, Pallas kernels for 0%

commit v1 on v0

--- a/solution.py
+++ b/solution.py
@@ -107,7 +107,9 @@
     grad_pooled = lax.psum_scatter(real_columns, "row", scatter_dimension=2, tiled=True)
     grad_pre_one = (unpool_columns(grad_pooled) * silu_slope(pre_one)).astype(jnp.bfloat16)
     local_one = tap_grads(grad_pre_one, padded_in)
-    grad_one = lax.psum(local_one, ("row", "col", "pair")) / math.sqrt(height * width)
+    grad_one = jnp.sum(lax.all_gather(local_one, ("row", "col", "pair")), axis=0) / math.sqrt(
+        height * width
+    )
     rimmed_one = padded_2(grad_pre_one, (("row", 1), (("col", "pair"), 2)), 1)
     input_grad = conv_valid(rimmed_one, flip_kernel(filters_one)).astype(jnp.bfloat16)
     return (input_grad, grad_one, grad_two)

time: 212 us -> 156 us (0.74)
  waiting for transfers between devices: 131 us -> 72.3 us
    psum x1 -> x0, waiting for transfers between devices: 91.9 us -> none  [local(): lax.psum(local_one, ('row', 'col', 'pair')) / math.sqrt(height * width)]
    all_gather x0 -> x1, waiting for transfers between devices: none -> 30.2 us  [local(): lax.all_gather(local_one, ('row', 'col', 'pair'))]
    reduce_sum x0 -> x1, other arithmetic: none -> 2.93 us  [local(): jnp.sum(lax.all_gather(local_one, ('row', 'col', 'pair')), axis=0)]
  transfers between devices with their start and end apart: 15 -> 15, of which waited for: 10 -> 11; matrix products, arithmetic and copies ran while one was open for 6% -> 8% of each run, Pallas kernels for 0% -> 0%
where the time goes in v1:
time: 156 us; the launch traced here: 155 us
  waiting for transfers between devices  72.3 us (46%)
  starting transfers between devices  27.7 us (18%)
  between operations  16.1 us (10%)
  blocking collectives  13.7 us (9%)
  other arithmetic  9.55 us (6%)
  local copies, waits for them, and re-layouts  8.38 us (5%)
  matrix products  7.49 us (5%)
    all_gather x1, waiting for transfers between devices, local(): lax.all_gather(local_one, ('row', 'col', 'pair'))  30.2 us
    ppermute x6, starting transfers between devices, padded_2(): lax.ppermute(tail, axis, [(i, (i + 1) % count) for i in range(ends)])  19.8 us
    reduce_scatter x1, waiting for transfers between devices, local(): lax.psum_scatter(real_columns, 'row', scatter_dimension=2, tiled=True)  18.7 us
    ppermute x6, waiting for transfers between devices, padded_2(): lax.ppermute(head, axis, [((i + 1) % count, i) for i in range(ends)])  14 us
    all_gather x1, blocking collectives, local(): column_strip = lax.all_gather(with_edges, 'row', axis=2, tiled=True)  13.7 us
    ppermute x6, starting transfers between devices, padded_2(): lax.ppermute(head, axis, [((i + 1) % count, i) for i in range(ends)])  7.75 us
    psum x1, waiting for transfers between devices, local(): lax.psum(local_two, ('col', 'pair'))  6.46 us
    unnamed x21, local copies, waits for them, and re-layouts  5.32 us
  transfers between devices with their start and end apart: 15, of which 11 were waited for; matrix products, arithmetic and copies ran while one was open for 8% of the time, Pallas kernels for 0%

profile of v1, /device:TPU:0, one launch (start us, length us, event | category | flops | bytes accessed | tf_op | source)
XLA Modules:
  0.0 155.2 jit_solution(4527058439460370187)
XLA Ops:
  8.1 1.0 copy.216
  9.1 4.9 %collective-permute-start = (bf16[64,1,128]{2,0,1:T(8,128)(2,1)S(1)}, bf16[64,1,128]{2,0,1:T(8,128)(2,1)S(1)}, u32[]{:S(2)}, u32[]{:S(2)}) collective-permute-start(bf16[64,1,128]{2,0,1:T(8,128)(2,1)S(1)} %get-tuple-element.58), channel_id=1, source_target_pairs={{0,4},{4,8},{8,12},{1,5},{5,9},{9,13},{2,6},{6,10},{10,14},{3,7},{... | collective-permute-start | bytes 49160 | tf_op jit(solution)/shard_map/ppermute | solution.py:16
  14.0 1.3 collective-permute-start.1
  15.4 0.9 constant_dynamic-update-slice_fusion.1
  16.4 3.3 %collective-permute-done.1 = bf16[64,1,128]{2,0,1:T(8,128)(2,1)S(1)} collective-permute-done((bf16[64,1,128]{2,0,1:T(8,128)(2,1)S(1)}, bf16[64,1,128]{2,0,1:T(8,128)(2,1)S(1)}, u32[]{:S(2)}, u32[]{:S(2)}) %collective-permute-start.1) | collective-permute-done | bytes 16416 | tf_op jit(solution)/shard_map/ppermute | solution.py:18
  19.7 1.3 collective-permute-start.3
  21.0 3.0 %collective-permute-start.2 = (bf16[64,10,1]{2,0,1:T(8,128)(2,1)S(1)}, bf16[64,10,1]{2,0,1:T(8,128)(2,1)S(1)}, u32[]{:S(2)}, u32[]{:S(2)}) collective-permute-start(bf16[64,10,1]{2,0,1:T(8,128)(2,1)S(1)} %get-tuple-element.51), channel_id=1, source_target_pairs={{0,1},{1,2},{2,3},{4,5},{5,6},{6,7},{8,9},{9,10},{10,11},{12,13},{... | collective-permute-start | bytes 3848 | tf_op jit(solution)/shard_map/ppermute | solution.py:16
  24.1 1.0 collective-permute-done.2
  26.5 0.8 convolution_select_fusion.1
  27.6 0.9 fusion.3
  28.8 1.3 collective-permute-start.5
  30.1 4.9 %collective-permute-start.4 = (bf16[256,1,2]{1,0,2:T(8,128)(2,1)S(1)}, bf16[256,1,2]{1,0,2:T(8,128)(2,1)S(1)}, u32[]{:S(2)}, u32[]{:S(2)}) collective-permute-start(bf16[256,1,2]{1,0,2:T(8,128)(2,1)S(1)} %get-tuple-element.55), channel_id=1, source_target_pairs={{0,1},{1,2},{2,3},{4,5},{5,6},{6,7},{8,9},{9,10},{10,11},{12,13},{... | collective-permute-start | bytes 3080 | tf_op jit(solution)/shard_map/ppermute | solution.py:16
  36.2 13.7 %all_gather.9 = bf16[256,34,8]{0,1,2:T(8,128)(2,1)S(1)} all-gather(bf16[256,34,2]{0,1,2:T(8,128)(2,1)S(1)} %copy.226), channel_id=1, replica_groups=mesh['grp'=2,'row'=4,'col'=2,'pair'=2] {'row'}, dimensions={2}, use_global_device_ids=true | all-gather | bytes 174080 | tf_op jit(solution)/shard_map/all_gather | solution.py:92
  50.1 1.0 fusion.6
  52.8 1.0 fusion.4
  53.8 2.5 %collective-permute-start.6 = (f32[256,1,8]{0,2,1:T(8,128)S(1)}, f32[256,1,8]{0,2,1:T(8,128)S(1)}, u32[]{:S(2)}, u32[]{:S(2)}) collective-permute-start(f32[256,1,8]{0,2,1:T(8,128)S(1)} %get-tuple-element.48), channel_id=1, source_target_pairs={{0,1},{1,2},{2,3},{4,5},{5,6},{6,7},{8,9},{9,10},{10,11},{12,13},{... | collective-permute-start | bytes 24584 | tf_op jit(solution)/shard_map/ppermute | solution.py:16
  56.5 1.3 collective-permute-start.7
  57.9 6.6 %collective-permute-done.7 = f32[256,1,8]{0,2,1:T(8,128)S(1)} collective-permute-done((f32[256,1,8]{0,2,1:T(8,128)S(1)}, f32[256,1,8]{0,2,1:T(8,128)S(1)}, u32[]{:S(2)}, u32[]{:S(2)}) %collective-permute-start.7) | collective-permute-done | bytes 8224 | tf_op jit(solution)/shard_map/ppermute | solution.py:18
  65.6 1.1 maximum_bitcast_fusion
  66.8 18.7 %reduce-scatter.2.cloned.1.call-done = f32[256,32,2]{0,1,2:T(8,128)} async-done(((f32[256,32,8]{0,1,2:T(8,128)}), f32[256,32,2]{0,1,2:T(8,128)}) %reduce-scatter.2.cloned.1.call-update) | async-done | bytes 65552 | tf_op jit(solution)/shard_map/reduce_scatter | solution.py:107
  85.5 0.8 broadcast_multiply_fusion.2
  90.1 1.3 collective-permute-start.8
  91.4 1.3 collective-permute-start.9
  93.0 4.2 %collective-permute-done.9 = bf16[64,1,128]{2,1,0:T(2,128)(2,1)S(1)} collective-permute-done((bf16[64,1,128]{2,1,0:T(2,128)(2,1)S(1)}, bf16[64,1,128]{2,1,0:T(2,128)(2,1)S(1)}, u32[]{:S(2)}, u32[]{:S(2)}) %collective-permute-start.9) | collective-permute-done | bytes 16416 | tf_op jit(solution)/shard_map/ppermute | solution.py:18
  97.4 1.3 collective-permute-start.11
  98.7 3.2 %collective-permute-start.10 = (bf16[64,10,1]{2,0,1:T(8,128)(2,1)S(1)}, bf16[64,10,1]{2,0,1:T(8,128)(2,1)S(1)}, u32[]{:S(2)}, u32[]{:S(2)}) collective-permute-start(bf16[64,10,1]{2,0,1:T(8,128)(2,1)S(1)} %get-tuple-element.49), channel_id=1, source_target_pairs={{0,1},{1,2},{2,3},{4,5},{5,6},{6,7},{8,9},{9,10},{10,11},{12,13},{... | collective-permute-start | bytes 3848 | tf_op jit(solution)/shard_map/ppermute | solution.py:16
  104.1 0.9 copy.259
  105.0 6.5 %all-reduce.4.cloned.1.call-done = f32[128,3,3,256]{3,0,1,2:T(8,128)} async-done(((f32[128,3,3,256]{3,0,1,2:T(8,128)}), f32[128,3,3,256]{3,0,1,2:T(8,128)}) %all-reduce.4.cloned.1.call-update) | async-done | bytes 1179664 | tf_op jit(solution)/shard_map/psum | solution.py:100
  111.4 1.4 broadcast_multiply_fusion
  112.8 1.1 copy.260
  113.9 30.2 %all-gather.3.cloned.1.call-done = f32[1024,3,3,64]{3,0,2,1:T(8,128)} async-done(((f32[64,3,3,64]{3,0,2,1:T(8,128)}), f32[1024,3,3,64]{3,0,2,1:T(8,128)}) %all-gather.3.cloned.1.call-update) | async-done | bytes 2359312 | tf_op jit(solution)/shard_map/all_gather | solution.py:110
  144.1 2.9 %reduce_sum.19 = f32[64,3,3,64]{3,0,2,1:T(8,128)S(1)} reduce(f32[16,64,3,3,64]{4,1,0,3,2:T(8,128)} %bitcast.143, f32[]{:T(128)} %constant.68.clone.1), dimensions={0}, to_apply=%region_2.3 | reduce | flops 552960 | bytes 2506756 | tf_op jit(solution)/shard_map/reduce_sum | solution.py:110
  (96 shorter events, 13.7 us)
Async XLA Ops:
  8.0 42.1 %copy-start = (bf16[128,3,3,256]{3,0,2,1:T(8,128)(2,1)S(1)}, bf16[128,3,3,256]{3,0,2,1:T(8,128)(2,1)}, u32[]{:S(2)}) copy-start(bf16[128,3,3,256]{3,0,2,1:T(8,128)(2,1)} %param.10) | copy-start | bytes 1769476
  8.0 77.5 %reduce-scatter.2.cloned.1.call-start = ((), (), s32[]{:S(2)}) async-start(), calls=%async_computation.1 | async-start | bytes 327680 | tf_op jit(solution)/shard_map/reduce_scatter | solution.py:107
  9.1 6.4 %collective-permute-start = (bf16[64,1,128]{2,0,1:T(8,128)(2,1)S(1)}, bf16[64,1,128]{2,0,1:T(8,128)(2,1)S(1)}, u32[]{:S(2)}, u32[]{:S(2)}) collective-permute-start(bf16[64,1,128]{2,0,1:T(8,128)(2,1)S(1)} %get-tuple-element.58), channel_id=1, source_target_pairs={{0,4},{4,8},{8,12},{1,5},{5,9},{9,13},{2,6},{6,10},{10,14},{3,7},{... | collective-permute-start | bytes 49160 | tf_op jit(solution)/shard_map/ppermute | solution.py:16
  14.0 5.6 %collective-permute-start.1 = (bf16[64,1,128]{2,0,1:T(8,128)(2,1)S(1)}, bf16[64,1,128]{2,0,1:T(8,128)(2,1)S(1)}, u32[]{:S(2)}, u32[]{:S(2)}) collective-permute-start(bf16[64,1,128]{2,0,1:T(8,128)(2,1)S(1)} %get-tuple-element.57), channel_id=1, source_target_pairs={{4,0},{8,4},{12,8},{5,1},{9,5},{13,9},{6,2},{10,6},{14,10},{7,3},{... | collective-permute-start | bytes 49160 | tf_op jit(solution)/shard_map/ppermute | solution.py:18
  19.7 4.4 %collective-permute-start.3 = (bf16[64,10,1]{2,0,1:T(8,128)(2,1)S(1)}, bf16[64,10,1]{2,0,1:T(8,128)(2,1)S(1)}, u32[]{:S(2)}, u32[]{:S(2)}) collective-permute-start(bf16[64,10,1]{2,0,1:T(8,128)(2,1)S(1)} %get-tuple-element.52), channel_id=1, source_target_pairs={{1,0},{2,1},{3,2},{5,4},{6,5},{7,6},{9,8},{10,9},{11,10},{13,12},{... | collective-permute-start | bytes 3848 | tf_op jit(solution)/shard_map/ppermute | solution.py:18
  21.0 4.0 %collective-permute-start.2 = (bf16[64,10,1]{2,0,1:T(8,128)(2,1)S(1)}, bf16[64,10,1]{2,0,1:T(8,128)(2,1)S(1)}, u32[]{:S(2)}, u32[]{:S(2)}) collective-permute-start(bf16[64,10,1]{2,0,1:T(8,128)(2,1)S(1)} %get-tuple-element.51), channel_id=1, source_target_pairs={{0,1},{1,2},{2,3},{4,5},{5,6},{6,7},{8,9},{9,10},{10,11},{12,13},{... | collective-permute-start | bytes 3848 | tf_op jit(solution)/shard_map/ppermute | solution.py:16
  25.6 0.9 copy-start.3
  25.6 0.9 copy-start.4
  28.8 6.4 %collective-permute-start.5 = (bf16[256,1,2]{1,0,2:T(8,128)(2,1)S(1)}, bf16[256,1,2]{1,0,2:T(8,128)(2,1)S(1)}, u32[]{:S(2)}, u32[]{:S(2)}) collective-permute-start(bf16[256,1,2]{1,0,2:T(8,128)(2,1)S(1)} %get-tuple-element.56), channel_id=1, source_target_pairs={{1,0},{2,1},{3,2},{5,4},{6,5},{7,6},{9,8},{10,9},{11,10},{13,12},{... | collective-permute-start | bytes 3080 | tf_op jit(solution)/shard_map/ppermute | solution.py:18
  30.1 5.8 %collective-permute-start.4 = (bf16[256,1,2]{1,0,2:T(8,128)(2,1)S(1)}, bf16[256,1,2]{1,0,2:T(8,128)(2,1)S(1)}, u32[]{:S(2)}, u32[]{:S(2)}) collective-permute-start(bf16[256,1,2]{1,0,2:T(8,128)(2,1)S(1)} %get-tuple-element.55), channel_id=1, source_target_pairs={{0,1},{1,2},{2,3},{4,5},{5,6},{6,7},{8,9},{9,10},{10,11},{12,13},{... | collective-permute-start | bytes 3080 | tf_op jit(solution)/shard_map/ppermute | solution.py:16
  50.1 1.0 copy-start.2
  53.8 4.0 %collective-permute-start.6 = (f32[256,1,8]{0,2,1:T(8,128)S(1)}, f32[256,1,8]{0,2,1:T(8,128)S(1)}, u32[]{:S(2)}, u32[]{:S(2)}) collective-permute-start(f32[256,1,8]{0,2,1:T(8,128)S(1)} %get-tuple-element.48), channel_id=1, source_target_pairs={{0,1},{1,2},{2,3},{4,5},{5,6},{6,7},{8,9},{9,10},{10,11},{12,13},{... | collective-permute-start | bytes 24584 | tf_op jit(solution)/shard_map/ppermute | solution.py:16
  56.5 7.9 %collective-permute-start.7 = (f32[256,1,8]{0,2,1:T(8,128)S(1)}, f32[256,1,8]{0,2,1:T(8,128)S(1)}, u32[]{:S(2)}, u32[]{:S(2)}) collective-permute-start(f32[256,1,8]{0,2,1:T(8,128)S(1)} %get-tuple-element.47), channel_id=1, source_target_pairs={{1,0},{2,1},{3,2},{5,4},{6,5},{7,6},{9,8},{10,9},{11,10},{13,12},{... | collective-permute-start | bytes 24584 | tf_op jit(solution)/shard_map/ppermute | solution.py:18
  65.2 46.2 %all-reduce.4.cloned.1.call-start = ((), (), s32[]{:S(2)}) async-start(), calls=%async_computation.2 | async-start | bytes 2359296 | tf_op jit(solution)/shard_map/psum | solution.py:100
  66.8 77.3 %all-gather.3.cloned.1.call-start = ((), (), s32[]{:S(2)}) async-start(), calls=%async_computation.3 | async-start | bytes 5013504 | tf_op jit(solution)/shard_map/all_gather | solution.py:110
  88.1 1.0 copy-start.1
  90.1 2.9 %collective-permute-start.8 = (bf16[64,1,128]{2,1,0:T(2,128)(2,1)S(1)}, bf16[64,1,128]{2,1,0:T(2,128)(2,1)S(1)}, u32[]{:S(2)}, u32[]{:S(2)}) collective-permute-start(bf16[64,1,128]{2,1,0:T(2,128)(2,1)S(1)} %get-tuple-element.54), channel_id=1, source_target_pairs={{0,4},{4,8},{8,12},{1,5},{5,9},{9,13},{2,6},{6,10},{10,14},{3,7},{... | collective-permute-start | bytes 49160 | tf_op jit(solution)/shard_map/ppermute | solution.py:16
  91.4 5.8 %collective-permute-start.9 = (bf16[64,1,128]{2,1,0:T(2,128)(2,1)S(1)}, bf16[64,1,128]{2,1,0:T(2,128)(2,1)S(1)}, u32[]{:S(2)}, u32[]{:S(2)}) collective-permute-start(bf16[64,1,128]{2,1,0:T(2,128)(2,1)S(1)} %get-tuple-element.53), channel_id=1, source_target_pairs={{4,0},{8,4},{12,8},{5,1},{9,5},{13,9},{6,2},{10,6},{14,10},{7,3},{... | collective-permute-start | bytes 49160 | tf_op jit(solution)/shard_map/ppermute | solution.py:18
  97.4 4.5 %collective-permute-start.11 = (bf16[64,10,1]{2,0,1:T(8,128)(2,1)S(1)}, bf16[64,10,1]{2,0,1:T(8,128)(2,1)S(1)}, u32[]{:S(2)}, u32[]{:S(2)}) collective-permute-start(bf16[64,10,1]{2,0,1:T(8,128)(2,1)S(1)} %get-tuple-element.50), channel_id=1, source_target_pairs={{1,0},{2,1},{3,2},{5,4},{6,5},{7,6},{9,8},{10,9},{11,10},{13,12},{... | collective-permute-start | bytes 3848 | tf_op jit(solution)/shard_map/ppermute | solution.py:18
  98.7 4.0 %collective-permute-start.10 = (bf16[64,10,1]{2,0,1:T(8,128)(2,1)S(1)}, bf16[64,10,1]{2,0,1:T(8,128)(2,1)S(1)}, u32[]{:S(2)}, u32[]{:S(2)}) collective-permute-start(bf16[64,10,1]{2,0,1:T(8,128)(2,1)S(1)} %get-tuple-element.49), channel_id=1, source_target_pairs={{0,1},{1,2},{2,3},{4,5},{5,6},{6,7},{8,9},{9,10},{10,11},{12,13},{... | collective-permute-start | bytes 3848 | tf_op jit(solution)/shard_map/ppermute | solution.py:16
Sparse Core Ops, SparseCore 0:
  65.4 20.0 reduce-scatter.1
  90.2 53.8 all-gather.2
Sparse Core Ops, SparseCore 1:
  68.8 42.6 all-reduce.3
